TPU v7x, 512 devices: a whole 4x8x8 slice. The times are simulated.
512 devices in a mesh: seq: 32 (over x, y), head: 16 (over z, core).
Axes of the slice: x: 4, y: 8, z: 8, core: 2. Of those that a mesh axis runs over, the one named last changes fastest.
Arguments:
- queries: bfloat16 [32768, 6144], P('seq', 'head'), may hold values from -64 to 64
- text: bfloat16 [512, 6144], P(None, 'seq'), may hold values from -6 to 6
- key_weight: bfloat16 [6144, 6144], P('seq', 'head'), may hold values from -0.078125 to 0.078125
- value_weight: bfloat16 [6144, 6144], P('seq', 'head'), may hold values from -0.078125 to 0.078125
- out_grad: bfloat16 [32768, 6144], P('seq', 'head'), may hold values from -6 to 6
Outputs:
- attn_out: bfloat16 [32768, 6144], P('seq', 'head')
- query_grad: bfloat16 [32768, 6144], P('seq', 'head')
- key_weight_grad: float32 [6144, 6144], P('seq', 'head')
- value_weight_grad: float32 [6144, 6144], P('seq', 'head')
- text_grad: float32 [512, 6144], P('head', 'seq')
All inputs are finite; a program needn't handle non-finite values.
Results may differ from a plain program's by a relative error of at most 0.006.
The roundings to bfloat16 on the way count: a program that leaves them out, or rounds other values in their place, can miss the bound.
Values may be sent and summed in bfloat16 or wider, within the bound.
A program may use at most 64 MiB of HBM per device.

v0:
```python
import jax
import jax.numpy as jnp
from jax import lax
from jax.sharding import PartitionSpec as P

HS = 128


def in_blocks(x, dim, devices):
    lengths = x.shape
    parts = x.reshape(*lengths[:dim], devices, lengths[dim] // devices, *lengths[dim + 1 :])
    return jnp.moveaxis(parts, dim, 0)


def summed_on_arrival(x, axis, dim):
    parts = in_blocks(x, dim, lax.axis_size(axis))
    arrived = lax.all_to_all(parts, axis, split_axis=0, concat_axis=0, tiled=True)
    return arrived.sum(axis=0)


def sent_to_all(x, axis):
    copies = jnp.broadcast_to(x, (lax.axis_size(axis), *x.shape))
    return lax.all_to_all(copies, axis, split_axis=0, concat_axis=0, tiled=True)


def in_order(parts, dim):
    parts = jnp.moveaxis(parts, 0, dim)
    lengths = parts.shape
    return parts.reshape(*lengths[:dim], lengths[dim] * lengths[dim + 1], *lengths[dim + 2 :])


def gathered_copies(x, axis, dim):
    parts = sent_to_all(x, axis)
    return in_order(parts, dim)


def in_one_piece(arrays, axis, dim, along):
    ends, at = ([], 0)
    for a in arrays[:-1]:
        at += a.shape[along]
        ends.append(at)
    both = jnp.concatenate(arrays, axis=along)
    return tuple(jnp.split(summed_on_arrival(both, axis, dim), ends, axis=along))


def in_one_piece_2(arrays, axis, dim, along):
    both = jnp.concatenate(arrays, axis=along)
    filled, at, finished = (lax.all_gather(both, axis, axis=dim, tiled=True), 0, [])
    for a in arrays:
        finished.append(lax.slice_in_dim(filled, at, at + a.shape[along], axis=along))
        at += a.shape[along]
    return tuple(finished)


def local(queries, text, key_weight, value_weight, out_grad):
    row_count = queries.shape[0]
    text_count = text.shape[0]
    head_count = key_weight.shape[1] // HS
    width = key_weight.shape[1]
    score_scale = 1.0 / HS**0.5
    shares = summed_on_arrival(
        jnp.concatenate(
            [
                jnp.dot(text, key_weight, preferred_element_type=jnp.float32),
                jnp.dot(text, value_weight, preferred_element_type=jnp.float32),
            ],
            axis=1,
        ),
        "seq",
        0,
    )
    shares_low = shares.astype(jnp.bfloat16)
    both_rows = gathered_copies(shares_low, "seq", 0)
    key_rows = both_rows[:, :width]
    value_rows = both_rows[:, width:]
    query_heads = queries.reshape(row_count, head_count, HS)
    grad_heads = out_grad.reshape(row_count, head_count, HS)
    key_heads = key_rows.reshape(text_count, head_count, HS)
    value_heads = value_rows.reshape(text_count, head_count, HS)
    scores = (
        jnp.einsum("rhd,thd->rht", query_heads, key_heads, preferred_element_type=jnp.float32)
        * score_scale
    )
    probs = jax.nn.softmax(scores, axis=-1)
    probs_low = probs.astype(jnp.bfloat16)
    attn_out = jnp.einsum(
        "rht,thd->rhd", probs_low, value_heads, preferred_element_type=jnp.float32
    )
    attn_out = attn_out.astype(jnp.bfloat16).reshape(row_count, width)
    dprobs = jnp.einsum("rhd,thd->rht", grad_heads, value_heads, preferred_element_type=jnp.float32)
    delta = jnp.sum(probs * dprobs, axis=-1, keepdims=True)
    dscores = (probs * (dprobs - delta) * score_scale).astype(jnp.bfloat16)
    key_term = jnp.einsum("rht,rhd->thd", dscores, query_heads, preferred_element_type=jnp.float32)
    value_term = jnp.einsum(
        "rht,rhd->thd", probs_low, grad_heads, preferred_element_type=jnp.float32
    )
    key_term = key_term.reshape(text_count, width)
    value_term = value_term.reshape(text_count, width)
    key_share, value_share = in_one_piece((key_term, value_term), "seq", 0, 1)
    key_grad, value_grad = in_one_piece_2(
        (key_share.astype(jnp.bfloat16), value_share.astype(jnp.bfloat16)), "seq", 0, 1
    )
    query_grad = jnp.einsum("rht,thd->rhd", dscores, key_heads, preferred_element_type=jnp.float32)
    query_grad = query_grad.astype(jnp.bfloat16).reshape(row_count, width)
    contract_rows = (((0,), (0,)), ((), ()))
    contract_cols = (((1,), (1,)), ((), ()))
    key_weight_grad = lax.dot_general(
        text, key_grad, contract_rows, preferred_element_type=jnp.float32
    )
    value_weight_grad = lax.dot_general(
        text, value_grad, contract_rows, preferred_element_type=jnp.float32
    )
    text_part = lax.dot_general(
        key_grad, key_weight, contract_cols, preferred_element_type=jnp.float32
    ) + lax.dot_general(value_grad, value_weight, contract_cols, preferred_element_type=jnp.float32)
    text_grad = summed_on_arrival(text_part, "head", 0)
    return (attn_out, query_grad, key_weight_grad, value_weight_grad, text_grad)


def solution(mesh):
    in_specs = (
        P("seq", "head"),
        P(None, "seq"),
        P("seq", "head"),
        P("seq", "head"),
        P("seq", "head"),
    )
    out_specs = (
        P("seq", "head"),
        P("seq", "head"),
        P("seq", "head"),
        P("seq", "head"),
        P("head", "seq"),
    )
    return jax.shard_map(local, mesh=mesh, in_specs=in_specs, out_specs=out_specs, check_vma=False)
```

profile of v0, /device:TPU:1, one launch (start us, length us, event | category | flops | bytes accessed | tf_op | source)
XLA Modules:
  0.0 235.0 jit_solution(2461614835769424964)
XLA Ops:
  0.6 0.0 copy-start
  0.6 0.9 copy-done
  1.6 1.2 fusion.40
  2.8 1.2 fusion.41
  4.0 0.1 pad_maximum_fusion
  4.2 0.5 copy.20
  4.6 46.9 %all_to_all.20 = f32[32,16,768]{2,1,0:T(8,128)S(1)} all-to-all(f32[32,16,768]{2,1,0:T(8,128)S(1)} %bitcast.80), channel_id=1, replica_groups=mesh['seq'=32,'head'=16] {'seq'}, dimensions={0} | all-to-all | bytes 3145728 | tf_op jit(solution)/shard_map/all_to_all | solution.py:17
  51.6 0.1 reduce_sum.45
  51.7 0.9 broadcast_in_dim.2
  52.6 8.1 %all-to-all-start.1 = ((bf16[32,16,768]{2,1,0:T(8,128)(2,1)}), bf16[32,16,768]{2,1,0:T(8,128)(2,1)S(1)}, u32[]{:S(2)}, u32[]{:S(2)}) async-start(bf16[32,16,768]{2,1,0:T(8,128)(2,1)} %broadcast_in_dim.2), calls=%async_computation.1 | async-start | bytes 1572864 | tf_op jit(solution)/shard_map/all_to_all | solution.py:23
  60.7 2.3 copy.23
  63.0 1.4 copy.27
  64.4 16.0 %all-to-all-done.1 = bf16[32,16,768]{2,1,0:T(8,128)(2,1)S(1)} async-done(((bf16[32,16,768]{2,1,0:T(8,128)(2,1)}), bf16[32,16,768]{2,1,0:T(8,128)(2,1)S(1)}, u32[]{:S(2)}, u32[]{:S(2)}) %all-to-all-start.1) | async-done | bytes 786464 | tf_op jit(solution)/shard_map/all_to_all | solution.py:23
  80.4 0.1 fusion.38
  80.5 0.0 copy-start.1
  80.5 0.9 copy.22
  81.4 0.0 copy-start.4
  81.4 0.2 copy.21
  81.6 3.7 %fusion.42 = f32[3,512,1024]{2,1,0:T(8,128)} fusion(bf16[512,3,128]{0,2,1:T(8,128)(2,1)S(1)} %bitcast.84, bf16[1024,3,128]{0,2,1:T(8,128)(2,1)S(1)} %bitcast.81), kind=kOutput, calls=%fused_computation.45 | convolution fusion | flops 402653184 | bytes 7471104 | tf_op jit(solution)/shard_map/rhd,thd->rht/dot_general | solution.py:90
  85.3 0.0 copy-done.1
  85.3 0.0 copy-done.4
  85.3 4.8 %fusion.39 = (f32[1024,3]{0,1:T(4,128)S(1)}, f32[1024,3,512]{0,2,1:T(8,128)}) fusion(bf16[512,3,128]{0,2,1:T(8,128)(2,1)S(1)} %bitcast.91, bf16[1024,3,128]{0,2,1:T(8,128)(2,1)S(1)} %bitcast.88), kind=kOutput, calls=%fused_computation.42 | convolution fusion | flops 407372288 | bytes 7483392 | tf_op jit(solution)/shard_map/sub | solution.py:84
  90.1 3.8 %fusion.22 = f32[512,3,128]{2,0,1:T(8,128)S(1)} fusion(bf16[1024,3,128]{0,2,1:T(8,128)(2,1)S(1)} %bitcast.82, f32[1024,3,512]{0,2,1:T(8,128)} %get-tuple-element.18, f32[1024,3]{0,1:T(4,128)S(1)} %get-tuple-element.17), kind=kOutput, calls=%fused_computation.25 | convolution fusion | flops 405798912 | bytes 7876608 | tf_op jit(solution)/shard_map/rht,rhd->thd/dot_general | solution.py:94
  93.9 11.0 %fusion.25 = f32[512,3,128]{2,0,1:T(8,128)S(1)} fusion(bf16[1024,3,128]{0,2,1:T(8,128)(2,1)} %bitcast.87, f32[3,512,1024]{2,1,0:T(8,128)} %fusion.42, f32[1024,3,512]{0,2,1:T(8,128)} %get-tuple-element.18, f32[1024,3]{0,1:T(4,128)S(1)} %get-tuple-element.17), kind=kOutput, calls=%fused_computation.26 | convolution fusion | flops 413666816 | bytes 14168064 | tf_op jit(solution)/shard_map/rht,rhd->thd/dot_general | solution.py:93
  104.9 0.5 copy.34
  105.4 0.4 concatenate.16
  105.9 0.5 copy.32
  106.4 0.4 concatenate.15
  106.8 1.4 pad_maximum_fusion.1
  108.2 7.9 %all-to-all-start.2 = ((f32[32,16,768]{2,1,0:T(8,128)}), f32[32,16,768]{2,1,0:T(8,128)S(1)}, u32[]{:S(2)}, u32[]{:S(2)}) async-start(f32[32,16,768]{2,1,0:T(8,128)} %pad_maximum_fusion.1), calls=%async_computation.2 | async-start | bytes 3145728 | tf_op jit(solution)/shard_map/all_to_all | solution.py:17
  116.2 0.0 copy-start.2
  116.2 0.0 copy-start.3
  116.2 3.4 %fusion.18 = bf16[3,128,1024]{2,1,0:T(8,128)(2,1)S(1)} fusion(bf16[512,3,128]{0,2,1:T(8,128)(2,1)S(1)} %bitcast.85, f32[1024,3,512]{0,2,1:T(8,128)} %get-tuple-element.18, f32[1024,3]{0,1:T(4,128)S(1)} %get-tuple-element.17), kind=kOutput, calls=%fused_computation.23 | convolution fusion | flops 406192128 | bytes 7483392 | tf_op jit(solution)/shard_map/rht,thd->rhd/dot_general | solution.py:86
  119.6 33.4 %all-to-all-done.2 = f32[32,16,768]{2,1,0:T(8,128)S(1)} async-done(((f32[32,16,768]{2,1,0:T(8,128)}), f32[32,16,768]{2,1,0:T(8,128)S(1)}, u32[]{:S(2)}, u32[]{:S(2)}) %all-to-all-start.2) | async-done | bytes 1572896 | tf_op jit(solution)/shard_map/all_to_all | solution.py:17
  153.0 0.1 reduce_sum.48
  153.0 37.7 %all_gather.3 = bf16[512,768]{1,0:T(8,128)(2,1)S(1)} all-gather(bf16[16,768]{1,0:T(8,128)(2,1)S(1)} %reduce_sum.48), channel_id=1, replica_groups=mesh['seq'=32,'head'=16] {'seq'}, dimensions={0}, use_global_device_ids=true | all-gather | bytes 811008 | tf_op jit(solution)/shard_map/all_gather | solution.py:48
  190.8 0.0 copy-done.2
  190.8 0.3 fusion.30
  191.1 0.0 copy-done.3
  191.1 0.3 convolution_add_fusion
  191.4 1.0 copy.35
  192.4 24.6 %all-to-all-start.3 = ((f32[16,32,192]{2,1,0:T(8,128)}), f32[16,32,192]{2,1,0:T(8,128)S(1)}, u32[]{:S(2)}, u32[]{:S(2)}) async-start(f32[16,32,192]{2,1,0:T(8,128)} %bitcast.16), calls=%async_computation.3 | async-start | bytes 1048576 | tf_op jit(solution)/shard_map/all_to_all | solution.py:17
  217.0 11.1 %fusion.21 = bf16[3,128,1024]{2,1,0:T(8,128)(2,1)S(1)} fusion(bf16[512,3,128]{0,2,1:T(8,128)(2,1)} %bitcast.90, f32[3,512,1024]{2,1,0:T(8,128)} %fusion.42, f32[1024,3,512]{0,2,1:T(8,128)} %get-tuple-element.18, f32[1024,3]{0,1:T(4,128)S(1)} %get-tuple-element.17), kind=kOutput, calls=%fused_computation.24 | convolution fusion | flops 414060032 | bytes 13774848 | tf_op jit(solution)/shard_map/rht,thd->rhd/dot_general | solution.py:103
  228.2 1.2 copy.37
  229.3 1.2 copy.36
  230.5 1.0 convolution_bitcast_fusion
  231.5 1.0 convolution_bitcast_fusion.1
  232.4 1.9 all-to-all-done.3
  234.4 0.7 reduce_sum.49
Async XLA Ops:
  0.6 0.9 copy-start
  52.6 27.8 %all-to-all-start.1 = ((bf16[32,16,768]{2,1,0:T(8,128)(2,1)}), bf16[32,16,768]{2,1,0:T(8,128)(2,1)S(1)}, u32[]{:S(2)}, u32[]{:S(2)}) async-start(bf16[32,16,768]{2,1,0:T(8,128)(2,1)} %broadcast_in_dim.2), calls=%async_computation.1 | async-start | bytes 1572864 | tf_op jit(solution)/shard_map/all_to_all | solution.py:23
  80.5 4.8 %copy-start.1 = (bf16[1024,384]{0,1:T(8,128)(2,1)S(1)}, bf16[1024,384]{0,1:T(8,128)(2,1)}, u32[]{:S(2)}) copy-start(bf16[1024,384]{0,1:T(8,128)(2,1)} %copy.23) | copy-start | bytes 2359300
  81.4 3.9 %copy-start.4 = (bf16[512,384]{0,1:T(8,128)(2,1)S(1)}, bf16[512,384]{0,1:T(8,128)(2,1)}, u32[]{:S(2)}) copy-start(bf16[512,384]{0,1:T(8,128)(2,1)} %copy.22) | copy-start | bytes 1179652
  108.2 44.7 %all-to-all-start.2 = ((f32[32,16,768]{2,1,0:T(8,128)}), f32[32,16,768]{2,1,0:T(8,128)S(1)}, u32[]{:S(2)}, u32[]{:S(2)}) async-start(f32[32,16,768]{2,1,0:T(8,128)} %pad_maximum_fusion.1), calls=%async_computation.2 | async-start | bytes 3145728 | tf_op jit(solution)/shard_map/all_to_all | solution.py:17
  116.2 74.6 %copy-start.2 = (bf16[192,384]{1,0:T(8,128)(2,1)S(1)}, bf16[192,384]{1,0:T(8,128)(2,1)}, u32[]{:S(2)}) copy-start(bf16[192,384]{1,0:T(8,128)(2,1)} %param.7) | copy-start | bytes 442372
  116.2 74.9 %copy-start.3 = (bf16[192,384]{1,0:T(8,128)(2,1)S(1)}, bf16[192,384]{1,0:T(8,128)(2,1)}, u32[]{:S(2)}) copy-start(bf16[192,384]{1,0:T(8,128)(2,1)} %param.8) | copy-start | bytes 442372
  192.4 41.9 %all-to-all-start.3 = ((f32[16,32,192]{2,1,0:T(8,128)}), f32[16,32,192]{2,1,0:T(8,128)S(1)}, u32[]{:S(2)}, u32[]{:S(2)}) async-start(f32[16,32,192]{2,1,0:T(8,128)} %bitcast.16), calls=%async_computation.3 | async-start | bytes 1048576 | tf_op jit(solution)/shard_map/all_to_all | solution.py:17
where the time goes:
time: 236 us; the launch traced here: 235 us
  blocking collectives  84.7 us (36%)
  waiting for transfers between devices  51.3 us (22%)
  matrix products  42.8 us (18%)
  starting transfers between devices  40.6 us (17%)
  local copies, waits for them, and re-layouts  12.5 us (5%)
    all_to_all x1, blocking collectives, summed_on_arrival(): lax.all_to_all(parts, axis, split_axis=0, concat_axis=0, tiled=True)  46.9 us
    all_gather x1, blocking collectives, in_one_piece_2(): lax.all_gather(both, axis, axis=dim, tiled=True)  37.7 us
    all_to_all x2, waiting for transfers between devices, summed_on_arrival(): lax.all_to_all(parts, axis, split_axis=0, concat_axis=0, tiled=True)  35.3 us
    all_to_all x2, starting transfers between devices, summed_on_arrival(): lax.all_to_all(parts, axis, split_axis=0, concat_axis=0, tiled=True)  32.5 us
    all_to_all x1, waiting for transfers between devices, sent_to_all(): return lax.all_to_all(copies, axis, split_axis=0, concat_axis=0, tiled=True)  16 us
    dot_general x1, matrix products, local(): jnp.einsum('rht,thd->rhd', dscores, key_heads, preferred_element_type=jnp...  11.1 us
    dot_general x1, matrix products, local(): jnp.einsum('rht,rhd->thd', dscores, query_heads, preferred_element_type=j...  11 us
    all_to_all x1, starting transfers between devices, sent_to_all(): return lax.all_to_all(copies, axis, split_axis=0, concat_axis=0, tiled=True)  8.08 us
  transfers between devices with their start and end apart: 3, of which 3 were waited for; matrix products, arithmetic and copies ran while one was open for 10% of the time, Pallas kernels for 0%

commit v1 on v0

v1 whole, which is shorter than its diff:
```python
import jax
import jax.numpy as jnp
from jax import lax
from jax.experimental import pallas as pl
from jax.experimental.pallas import tpu as pltpu
from jax.sharding import PartitionSpec as P

MESH = pl.DeviceIdType.MESH
NX, NY, NZ, NC = 4, 8, 8, 2
HS = 128
HEADS = 3
TEXT = 512
FEAT = 192
ROWS = 1024
XT = TEXT // NX
YT = XT // NY
ZT = TEXT // (NZ * NC)
RB = 256
NB = ROWS // RB
SCALE = 1.0 / HS**0.5
EXP2_SCALE = SCALE * 1.4426950408889634
BF = jnp.bfloat16
F32 = jnp.float32

S_KX, S_VX, S_KY, S_VY, S_AY, S_AX, S_GX, S_GY, S_GAY, S_GAX = range(10)


def dot(a, b):
    return jnp.dot(a, b, preferred_element_type=F32)


def kernel(
    q_hbm, tt_hbm, kw_hbm, vw_hbm, og_hbm,
    o_hbm, dq_hbm, kwg_hbm, vwg_hbm, tg_hbm,
    q_v, og_v, text_v, kw_v, vw_v, w_v,
    qt_v, ogt_v, tt_v, kt_v, vt_v,
    kp, vp, kx, vx, ks, vs, ky, vy, kvf,
    dk_acc, dv_acc, gp, gx, gs, gy, gf,
    o_v, dq_v, kwg_v, vwg_v, tp, tc, ts, tz, tg_v,
    in_sem, out_sem, ssem, rsem, fs_sem, fr_sem,
):
    seq = lax.axis_index("seq")
    head = lax.axis_index("head")
    mx, my = seq // NY, lax.rem(seq, NY)
    mz, mc = head // NC, lax.rem(head, NC)

    def x_peer(i):
        px = lax.rem(mx + i, NX)
        return px, (px * NY + my, head)

    def y_peer(i):
        py = lax.rem(my + i, NY)
        return py, (mx * NY + py, head)

    def z_peer(i):
        pz = lax.rem(mz + i, NZ)
        return pz, (seq, pz * NC + mc)

    core_peer = (seq, mz * NC + (1 - mc))

    barrier = pltpu.get_barrier_semaphore()
    peers = [x_peer(i)[1] for i in range(1, NX)] + [y_peer(i)[1] for i in range(1, NY)]
    peers += [z_peer(i)[1] for i in range(1, NZ)] + [core_peer]
    for peer in peers:
        pl.semaphore_signal(barrier, inc=1, device_id=peer, device_id_type=MESH)

    loads = [
        pltpu.make_async_copy(a, b, in_sem.at[i])
        for i, (a, b) in enumerate(
            ((tt_hbm, tt_v), (kw_hbm, kw_v), (vw_hbm, vw_v), (q_hbm, q_v), (og_hbm, og_v))
        )
    ]
    for load in loads:
        load.start()

    def send(src, dst, h, stage, device):
        pltpu.make_async_remote_copy(
            src_ref=src, dst_ref=dst, send_sem=ssem.at[h, stage], recv_sem=rsem.at[h, stage],
            device_id=device, device_id_type=MESH,
        ).start()

    def bytes_of(h, stage):
        return {
            S_KX: kx.at[h, pl.ds(0, NX - 1)],
            S_VX: vx.at[h, pl.ds(0, NX - 1)],
            S_KY: ky.at[h, pl.ds(0, NY - 1)],
            S_VY: vy.at[h, pl.ds(0, NY - 1)],
            S_AY: kvf.at[h, 0, pl.ds(0, NY - 1)],
            S_AX: kvf.at[h, pl.ds(0, NX - 1)],
            S_GX: gx.at[h, pl.ds(0, NX - 1)],
            S_GY: gy.at[h, pl.ds(0, NY - 1)],
            S_GAY: gf.at[h, 0, pl.ds(0, NY - 1)],
            S_GAX: gf.at[h, pl.ds(0, NX - 1)],
        }[stage]

    def wait(sem, h, stage):
        ref = bytes_of(h, stage)
        pltpu.make_async_copy(ref, ref, sem.at[h, stage]).wait()

    def project(h):
        cols = slice(h * HS, (h + 1) * HS)
        kp[h] = dot(text_v[...], kw_v[:, cols]).reshape(NX, NY, YT, HS)
        vp[h] = dot(text_v[...], vw_v[:, cols]).astype(BF).reshape(NX, NY, YT, HS)

    def f_x(h):
        for i in (2, 1, 3):
            px, device = x_peer(i)
            send(kp.at[h, px], kx.at[h, mx], h, S_KX, device)
            send(vp.at[h, px], vx.at[h, mx], h, S_VX, device)

    def f_y(h):
        wait(rsem, h, S_KX)
        wait(rsem, h, S_VX)
        k = kp[h, mx]
        v = vp[h, mx].astype(F32)
        for i in range(1, NX):
            k = k + kx[h, x_peer(i)[0]]
            v = v + vx[h, x_peer(i)[0]].astype(F32)
        ks[h] = k
        vs[h] = v.astype(BF)
        for i in (4, 3, 5, 2, 6, 1, 7):
            py, device = y_peer(i)
            send(ks.at[h, py], ky.at[h, my], h, S_KY, device)
            send(vs.at[h, py], vy.at[h, my], h, S_VY, device)

    def f_ay(h):
        wait(rsem, h, S_KY)
        wait(rsem, h, S_VY)
        k = ks[h, my]
        v = vs[h, my].astype(F32)
        for i in range(1, NY):
            k = k + ky[h, y_peer(i)[0]]
            v = v + vy[h, y_peer(i)[0]].astype(F32)
        kvf[h, mx, my, :, :HS] = k.astype(BF)
        kvf[h, mx, my, :, HS:] = v.astype(BF)
        for i in (4, 3, 5, 2, 6, 1, 7):
            send(kvf.at[h, mx, my], kvf.at[h, mx, my], h, S_AY, y_peer(i)[1])

    def f_ax(h):
        wait(rsem, h, S_AY)
        for i in (2, 1, 3):
            send(kvf.at[h, mx], kvf.at[h, mx], h, S_AX, x_peer(i)[1])

    def attend(h):
        wait(rsem, h, S_AX)
        cols = slice(h * HS, (h + 1) * HS)
        kt_v[...] = kvf[h, :, :, :, :HS].reshape(TEXT, HS).T
        vt_v[...] = kvf[h, :, :, :, HS:].reshape(TEXT, HS).T
        dk_acc[...] = jnp.zeros_like(dk_acc)
        dv_acc[...] = jnp.zeros_like(dv_acc)

        def block(b, carry):
            rows = pl.ds(pl.multiple_of(b * RB, RB), RB)
            k = kvf[h, :, :, :, :HS].reshape(TEXT, HS)
            v = kvf[h, :, :, :, HS:].reshape(TEXT, HS)
            s = dot(k, qt_v[h, b])
            e = jnp.exp2((s - jnp.max(s, axis=0, keepdims=True)) * EXP2_SCALE)
            p = e * (1.0 / jnp.sum(e, axis=0, keepdims=True))
            low = p.astype(BF)
            o_v[h, rows, :] = dot(vt_v[...], low).T.astype(BF)
            dp = dot(v, ogt_v[h, b])
            delta = jnp.sum(p * dp, axis=0, keepdims=True)
            ds = (p * (dp - delta) * SCALE).astype(BF)
            dq_v[h, rows, :] = dot(kt_v[...], ds).T.astype(BF)
            dk_acc[...] += dot(ds, q_v[rows, cols])
            dv_acc[...] += dot(low, og_v[rows, cols])
            return carry

        lax.fori_loop(0, NB, block, 0)
        for i, (a, b) in enumerate(((o_v, o_hbm), (dq_v, dq_hbm))):
            pltpu.make_async_copy(a.at[h], b.at[:, pl.ds(h * HS, HS)], out_sem.at[h, i]).start()
        gp[h, :, :, :, :HS] = dk_acc[...].astype(BF).reshape(NX, NY, YT, HS)
        gp[h, :, :, :, HS:] = dv_acc[...].astype(BF).reshape(NX, NY, YT, HS)
        for i in (2, 1, 3):
            px, device = x_peer(i)
            send(gp.at[h, px], gx.at[h, mx], h, S_GX, device)

    def b_y(h):
        wait(rsem, h, S_GX)
        g = gp[h, mx].astype(F32)
        for i in range(1, NX):
            g = g + gx[h, x_peer(i)[0]].astype(F32)
        gs[h] = g.astype(BF)
        for i in (4, 3, 5, 2, 6, 1, 7):
            py, device = y_peer(i)
            send(gs.at[h, py], gy.at[h, my], h, S_GY, device)

    def b_ay(h):
        wait(rsem, h, S_GY)
        g = gs[h, my].astype(F32)
        for i in range(1, NY):
            g = g + gy[h, y_peer(i)[0]].astype(F32)
        gf[h, mx, my] = g.astype(BF)
        for i in (4, 3, 5, 2, 6, 1, 7):
            send(gf.at[h, mx, my], gf.at[h, mx, my], h, S_GAY, y_peer(i)[1])

    def b_ax(h):
        wait(rsem, h, S_GAY)
        for i in (2, 1, 3):
            send(gf.at[h, mx], gf.at[h, mx], h, S_GAX, x_peer(i)[1])

    def finish(h):
        wait(rsem, h, S_GAX)
        cols = slice(h * HS, (h + 1) * HS)
        g = gf[h].reshape(TEXT, 2 * HS)
        part = lax.dot_general(g, w_v[h], (((1,), (1,)), ((), ())), preferred_element_type=F32)
        part = part.reshape(NZ, NC, ZT, FEAT)
        if h == 0:
            tp[...] = part
        else:
            tp[...] += part
        if h == HEADS - 1:
            pltpu.make_async_remote_copy(
                src_ref=tp.at[:, 1 - mc], dst_ref=tc, send_sem=fs_sem.at[0], recv_sem=fr_sem.at[0],
                device_id=core_peer, device_id_type=MESH,
            ).start()
        wg = dot(tt_v[...], g)
        kwg_v[:, cols] = wg[:, :HS]
        vwg_v[:, cols] = wg[:, HS:]

    for i in range(3):
        loads[i].wait()
    text_v[...] = tt_v[...].T
    for h in range(HEADS):
        project(h)
        if h == 0:
            pl.semaphore_wait(barrier, len(peers))
        f_x(h)
    for i in range(3, 5):
        loads[i].wait()
    for h in range(HEADS):
        cols = slice(h * HS, (h + 1) * HS)
        w_v[h, :, :HS] = kw_v[:, cols]
        w_v[h, :, HS:] = vw_v[:, cols]

        def turn(b, carry, h=h, cols=cols):
            rows = pl.ds(pl.multiple_of(b * RB, RB), RB)
            qt_v[h, b] = q_v[rows, cols].T
            ogt_v[h, b] = og_v[rows, cols].T
            return carry

        lax.fori_loop(0, NB, turn, 0)
    f_y(0)
    f_y(1)
    f_ay(0)
    f_y(2)
    f_ay(1)
    f_ax(0)
    f_ay(2)
    f_ax(1)
    f_ax(2)
    attend(0)
    attend(1)
    b_y(0)
    attend(2)
    b_ay(0)
    b_y(1)
    b_ax(0)
    b_ay(1)
    b_y(2)
    b_ax(1)
    b_ay(2)
    finish(0)
    b_ax(2)
    finish(1)
    finish(2)

    pltpu.make_async_copy(kwg_v, kwg_hbm, out_sem.at[HEADS, 0]).start()
    pltpu.make_async_copy(vwg_v, vwg_hbm, out_sem.at[HEADS, 1]).start()

    def final_wait(sem, i, ref):
        pltpu.make_async_copy(ref, ref, sem.at[i]).wait()

    final_wait(fr_sem, 0, tc)
    ts[...] = (tp[:, mc] + tc[...]).astype(BF)
    for i in (4, 3, 5, 2, 6, 1, 7):
        pz, device = z_peer(i)
        pltpu.make_async_remote_copy(
            src_ref=ts.at[pz], dst_ref=tz.at[mz], send_sem=fs_sem.at[1], recv_sem=fr_sem.at[1],
            device_id=device, device_id_type=MESH,
        ).start()
    for h in range(HEADS):
        for stage in range(10):
            wait(ssem, h, stage)
        for i, (a, b) in enumerate(((o_v, o_hbm), (dq_v, dq_hbm))):
            pltpu.make_async_copy(a.at[h], b.at[:, pl.ds(h * HS, HS)], out_sem.at[h, i]).wait()
    final_wait(fs_sem, 0, tc)
    final_wait(fr_sem, 1, tz.at[pl.ds(0, NZ - 1)])
    t = tp[mz, mc] + tc[mz]
    for i in range(1, NZ):
        t = t + tz[z_peer(i)[0]].astype(F32)
    tg_v[...] = t
    last = pltpu.make_async_copy(tg_v, tg_hbm, out_sem.at[HEADS, 2])
    last.start()
    pltpu.make_async_copy(kwg_v, kwg_hbm, out_sem.at[HEADS, 0]).wait()
    pltpu.make_async_copy(vwg_v, vwg_hbm, out_sem.at[HEADS, 1]).wait()
    final_wait(fs_sem, 1, tz.at[pl.ds(0, NZ - 1)])
    last.wait()


def local(queries, text, key_weight, value_weight, out_grad):
    width = HEADS * HS
    vm = pltpu.VMEM
    dma = pltpu.SemaphoreType.DMA
    return pl.pallas_call(
        kernel,
        name="cross_attention",
        out_shape=(
            jax.ShapeDtypeStruct((ROWS, width), BF),
            jax.ShapeDtypeStruct((ROWS, width), BF),
            jax.ShapeDtypeStruct((FEAT, width), F32),
            jax.ShapeDtypeStruct((FEAT, width), F32),
            jax.ShapeDtypeStruct((ZT, FEAT), F32),
        ),
        in_specs=[pl.BlockSpec(memory_space=pl.ANY)] * 5,
        out_specs=tuple([pl.BlockSpec(memory_space=pl.ANY)] * 5),
        scratch_shapes=[
            vm((ROWS, width), BF), vm((ROWS, width), BF), vm((TEXT, FEAT), BF),
            vm((FEAT, width), BF), vm((FEAT, width), BF), vm((HEADS, FEAT, 2 * HS), BF),
            vm((HEADS, NB, HS, RB), BF), vm((HEADS, NB, HS, RB), BF), vm((FEAT, TEXT), BF),
            vm((HS, TEXT), BF), vm((HS, TEXT), BF),
            vm((HEADS, NX, NY, YT, HS), F32), vm((HEADS, NX, NY, YT, HS), BF),
            vm((HEADS, NX, NY, YT, HS), F32), vm((HEADS, NX, NY, YT, HS), BF),
            vm((HEADS, NY, YT, HS), F32), vm((HEADS, NY, YT, HS), BF),
            vm((HEADS, NY, YT, HS), F32), vm((HEADS, NY, YT, HS), BF),
            vm((HEADS, NX, NY, YT, 2 * HS), BF),
            vm((TEXT, HS), F32), vm((TEXT, HS), F32),
            vm((HEADS, NX, NY, YT, 2 * HS), BF), vm((HEADS, NX, NY, YT, 2 * HS), BF),
            vm((HEADS, NY, YT, 2 * HS), BF), vm((HEADS, NY, YT, 2 * HS), BF),
            vm((HEADS, NX, NY, YT, 2 * HS), BF),
            vm((HEADS, ROWS, HS), BF), vm((HEADS, ROWS, HS), BF),
            vm((FEAT, width), F32), vm((FEAT, width), F32),
            vm((NZ, NC, ZT, FEAT), F32), vm((NZ, ZT, FEAT), F32),
            vm((NZ, ZT, FEAT), BF), vm((NZ, ZT, FEAT), BF), vm((ZT, FEAT), F32),
            dma((5,)), dma((HEADS + 1, 3)), dma((HEADS, 10)), dma((HEADS, 10)), dma((2,)), dma((2,)),
        ],
        compiler_params=pltpu.CompilerParams(
            collective_id=0, has_side_effects=True, vmem_limit_bytes=56 * 1024 * 1024
        ),
    )(queries, text.T, key_weight, value_weight, out_grad)


def solution(mesh):
    in_specs = (
        P("seq", "head"),
        P(None, "seq"),
        P("seq", "head"),
        P("seq", "head"),
        P("seq", "head"),
    )
    out_specs = (
        P("seq", "head"),
        P("seq", "head"),
        P("seq", "head"),
        P("seq", "head"),
        P("head", "seq"),
    )
    return jax.shard_map(local, mesh=mesh, in_specs=in_specs, out_specs=out_specs, check_vma=False)
```

time: 236 us -> 90.2 us (0.38)
  blocking collectives: 84.7 us -> 0 us
  Pallas kernels: 0 us -> 83.5 us
  waiting for transfers between devices: 51.3 us -> 0 us
  matrix products: 42.8 us -> 0 us
  starting transfers between devices: 40.6 us -> 0 us
  local copies, waits for them, and re-layouts: 12.5 us -> 5.73 us
    pallas_call x0 -> x1, Pallas kernels: none -> 83.5 us  [local(): pl.pallas_call(kernel, name='cross_attention', out_shape=(jax.ShapeDtypeS...]
    all_to_all x3 -> x0, waiting for transfers between devices: 51.3 us -> none  [the longest x2 35.3 us: summed_on_arrival(): lax.all_to_all(parts, axis, split_axis=0, concat_axis=0, tiled=True)]
    all_to_all x1 -> x0, blocking collectives: 46.9 us -> none  [summed_on_arrival(): lax.all_to_all(parts, axis, split_axis=0, concat_axis=0, tiled=True)]
    all_to_all x3 -> x0, starting transfers between devices: 40.6 us -> none  [the longest x2 32.5 us: summed_on_arrival(): lax.all_to_all(parts, axis, split_axis=0, concat_axis=0, tiled=True)]
    dot_general x11 -> x0, matrix products: 38 us -> none  [the longest x1 11.1 us: local(): jnp.einsum('rht,thd->rhd', dscores, key_heads, preferred_element_type=jnp...]
    all_gather x1 -> x0, blocking collectives: 37.7 us -> none  [in_one_piece_2(): lax.all_gather(both, axis, axis=dim, tiled=True)]
    sub x1 -> x0, matrix products: 4.82 us -> none  [local(): probs = jax.nn.softmax(scores, axis=-1)]
    unnamed x14 -> x13, local copies, waits for them, and re-layouts: 6.95 us -> 5.73 us
  transfers between devices with their start and end apart: 3 -> 0, of which waited for: 3 -> 0; matrix products, arithmetic and copies ran while one was open for 10% -> 0% of each run, Pallas kernels for 0% -> 0%
where the time goes in v1:
time: 90.2 us; the launch traced here: 89.9 us
  Pallas kernels  83.5 us (93%)
  local copies, waits for them, and re-layouts  5.73 us (6%)
    pallas_call x1, Pallas kernels, local(): pl.pallas_call(kernel, name='cross_attention', out_shape=(jax.ShapeDtypeS...  83.5 us
    unnamed x13, local copies, waits for them, and re-layouts  5.73 us

profile of v1, /device:TPU:1, one launch (start us, length us, event | category | flops | bytes accessed | tf_op | source)
XLA Modules:
  0.0 89.9 jit_solution(9679006012719764231)
XLA Ops:
  0.6 83.5 %cross_attention.1 = (bf16[1024,384]{1,0:T(8,128)(2,1)}, bf16[1024,384]{1,0:T(8,128)(2,1)}, f32[192,384]{1,0:T(8,128)}, f32[192,384]{1,0:T(8,128)}, f32[32,192]{1,0:T(8,128)}) custom-call(bf16[1024,384]{1,0:T(8,128)(2,1)} %q_hbm.1, bf16[192,512]{1,0:T(8,128)(2,1)} %bitcast.1, bf16[192,384]{1,0:T(8,128)(2,1)} %kw_hbm.1, bf16[192,384]{1,0:T(8,128)(2,1)} %vw_hbm.1, ...), custom_call_target="tpu_custom_call" | custom-call | tf_op jit(solution)/shard_map/cross_attention/pallas_call | solution.py:305
  84.1 0.0 copy-start
  84.1 2.2 %copy.15 = bf16[1024,384]{1,0:T(8,128)(2,1)} copy(bf16[1024,384]{1,0:T(8,128)(2,1)} %get-tuple-element.10) | data formatting | bytes 1572864
  86.3 0.0 copy-done
  86.3 0.0 copy-start.2
  86.3 0.9 copy.16
  87.2 0.2 copy-done.2
  87.4 0.0 copy-start.1
  87.4 0.7 copy.17
  88.1 0.4 copy-done.1
  88.5 0.0 copy-start.3
  88.5 0.7 copy.18
  89.2 0.0 copy-done.3
  89.2 0.6 copy.19
Async XLA Ops:
  84.1 2.2 %copy-start = (bf16[1024,384]{1,0:T(8,128)(2,1)S(1)}, bf16[1024,384]{1,0:T(8,128)(2,1)}, u32[]{:S(2)}) copy-start(bf16[1024,384]{1,0:T(8,128)(2,1)} %get-tuple-element.11) | copy-start | bytes 2359300
  86.3 1.1 %copy-start.2 = (f32[192,384]{1,0:T(8,128)S(1)}, f32[192,384]{1,0:T(8,128)}, u32[]{:S(2)}) copy-start(f32[192,384]{1,0:T(8,128)} %get-tuple-element.12) | copy-start | bytes 884740
  87.4 1.1 %copy-start.1 = (f32[192,384]{1,0:T(8,128)S(1)}, f32[192,384]{1,0:T(8,128)}, u32[]{:S(2)}) copy-start(f32[192,384]{1,0:T(8,128)} %get-tuple-element.13) | copy-start | bytes 884740
  88.5 0.8 copy-start.3

commit v2 on v1

v2 whole, which is shorter than its diff:
```python
import jax
import jax.numpy as jnp
from jax import lax
from jax.experimental import pallas as pl
from jax.experimental.pallas import tpu as pltpu
from jax.sharding import PartitionSpec as P

MESH = pl.DeviceIdType.MESH
NX, NY, NZ, NC = 4, 8, 8, 2
HS = 128
HEADS = 3
TEXT = 512
FEAT = 192
ROWS = 1024
TH = TEXT // 2
YT = TH // NY
FH = FEAT // 2
ZT = TEXT // (NZ * NC)
SCALE = 1.0 / HS**0.5
EXP2_SCALE = SCALE * 1.4426950408889634
BF = jnp.bfloat16
F32 = jnp.float32

S_W, S_Y, S_AY, S_AX, S_GX, S_GY, S_GAY, S_GAX = range(8)
FAR_FIRST = (4, 3, 5, 2, 6, 1, 7)


def dot(a, b):
    return jnp.dot(a, b, preferred_element_type=F32)


def kernel(
    q_hbm, tt_hbm, kw_hbm, vw_hbm, og_hbm,
    o_ref, dq_ref, kwg_ref, vwg_ref, tg_ref,
    q_v, og_v, tt_v, w_v, tx, wx, txt, qt_v, ogt_v,
    ks, ky, kvf, gp, gx, gs, gy, gf,
    tp, tc, ts, tz,
    in_sem, ssem, rsem, fs_sem, fr_sem,
):
    seq = lax.axis_index("seq")
    head = lax.axis_index("head")
    mx, my = seq // NY, lax.rem(seq, NY)
    mz, mc = head // NC, lax.rem(head, NC)
    mb, ma = mx // 2, lax.rem(mx, 2)

    def x_peer(i):
        px = lax.rem(mx + i, NX)
        return px, (px * NY + my, head)

    def y_peer(i):
        py = lax.rem(my + i, NY)
        return py, (mx * NY + py, head)

    def z_peer(i):
        pz = lax.rem(mz + i, NZ)
        return pz, (seq, pz * NC + mc)

    core_peer = (seq, mz * NC + (1 - mc))

    barrier = pltpu.get_barrier_semaphore()
    peers = [x_peer(i)[1] for i in range(1, NX)] + [y_peer(i)[1] for i in range(1, NY)]
    peers += [z_peer(i)[1] for i in range(1, NZ)] + [core_peer]
    for peer in peers:
        pl.semaphore_signal(barrier, inc=1, device_id=peer, device_id_type=MESH)

    loads = []
    for a in range(2):
        for c in range(NC):
            loads.append((tt_hbm.at[pl.ds(c * FH, FH), pl.ds(a * TH, TH)], tt_v.at[a, c]))
    for h in range(HEADS):
        loads.append((kw_hbm.at[:, pl.ds(h * HS, HS)], w_v.at[0, h]))
        loads.append((vw_hbm.at[:, pl.ds(h * HS, HS)], w_v.at[1, h]))
    loads += [(q_hbm, q_v), (og_hbm, og_v)]
    loads = [pltpu.make_async_copy(a, b, in_sem.at[i]) for i, (a, b) in enumerate(loads)]
    for load in loads:
        load.start()

    def copy_to(src, dst, s_sem, r_sem, device):
        pltpu.make_async_remote_copy(
            src_ref=src, dst_ref=dst, send_sem=s_sem, recv_sem=r_sem,
            device_id=device, device_id_type=MESH,
        ).start()

    def send(src, dst, h, stage, device):
        copy_to(src, dst, ssem.at[h, stage], rsem.at[h, stage], device)

    def wait_bytes(sem, ref):
        pltpu.make_async_copy(ref, ref, sem).wait()

    def wait(sem, h, stage):
        ref = {
            S_W: wx.at[h, pl.ds(0, NX - 1)],
            S_Y: ky.at[h, pl.ds(0, NY - 1)],
            S_AY: kvf.at[h, 0, pl.ds(0, NY - 1)],
            S_AX: kvf.at[h, pl.ds(0, NX - 1)],
            S_GX: gx.at[h, pl.ds(0, NX - 1)],
            S_GY: gy.at[h, pl.ds(0, NY - 1)],
            S_GAY: gf.at[h, 0, pl.ds(0, NY - 1)],
            S_GAX: gf.at[h, pl.ds(0, NX - 1)],
        }[stage]
        wait_bytes(sem.at[h, stage], ref)

    def spread_y(full, h, stage):
        for i in FAR_FIRST:
            send(full.at[h, mx, my], full.at[h, mx, my], h, stage, y_peer(i)[1])

    def spread_x(full, h, before, stage):
        wait(rsem, h, before)
        for i in (2, 1, 3):
            send(full.at[h, mx], full.at[h, mx], h, stage, x_peer(i)[1])

    def f_w(h):
        for i in (2, 1, 3):
            px, device = x_peer(i)
            send(w_v.at[px // 2, h], wx.at[h, mx], h, S_W, device)

    def f_y(h):
        wait(rsem, h, S_W)
        p = dot(txt[mx], w_v[mb, h])
        for i in range(1, NX):
            px = x_peer(i)[0]
            p = p + dot(txt[px], wx[h, px])
        ks[h] = p.reshape(NY, YT, HS)
        for i in FAR_FIRST:
            py, device = y_peer(i)
            send(ks.at[h, py], ky.at[h, my], h, S_Y, device)

    def f_ay(h):
        wait(rsem, h, S_Y)
        k = ks[h, my]
        for i in range(1, NY):
            k = k + ky[h, y_peer(i)[0]]
        kvf[h, mx, my] = k.astype(BF)
        spread_y(kvf, h, S_AY)

    def f_ax(h):
        spread_x(kvf, h, S_AY, S_AX)

    def attend(h):
        wait(rsem, h, S_AX)
        cols = slice(h * HS, (h + 1) * HS)
        k = kvf[h, 0:2].reshape(TEXT, HS)
        v = kvf[h, 2:4].reshape(TEXT, HS)
        s = dot(k, qt_v[h])
        e = jnp.exp2((s - jnp.max(s, axis=0, keepdims=True)) * EXP2_SCALE)
        p = e * (1.0 / jnp.sum(e, axis=0, keepdims=True))
        low = p.astype(BF)
        dp = dot(v, ogt_v[h])
        delta = jnp.sum(p * dp, axis=0, keepdims=True)
        ds = (p * (dp - delta) * SCALE).astype(BF)
        gp[h, 2:4] = dot(low, og_v[:, cols]).astype(BF).reshape(2, NY, YT, HS)
        gp[h, 0:2] = dot(ds, q_v[:, cols]).astype(BF).reshape(2, NY, YT, HS)
        for i in (2, 1, 3):
            px, device = x_peer(i)
            send(gp.at[h, px], gx.at[h, mx], h, S_GX, device)
        o_ref[:, cols] = dot(v.T, low).T.astype(BF)
        dq_ref[:, cols] = dot(k.T, ds).T.astype(BF)

    def b_y(h):
        wait(rsem, h, S_GX)
        g = gp[h, mx].astype(F32)
        for i in range(1, NX):
            g = g + gx[h, x_peer(i)[0]].astype(F32)
        gs[h] = g.astype(BF)
        for i in FAR_FIRST:
            py, device = y_peer(i)
            send(gs.at[h, py], gy.at[h, my], h, S_GY, device)

    def b_ay(h):
        wait(rsem, h, S_GY)
        g = gs[h, my].astype(F32)
        for i in range(1, NY):
            g = g + gy[h, y_peer(i)[0]].astype(F32)
        gf[h, mx, my] = g.astype(BF)
        spread_y(gf, h, S_GAY)

    def b_ax(h):
        spread_x(gf, h, S_GAY, S_GAX)

    def finish(h):
        wait(rsem, h, S_GAX)
        cols = slice(h * HS, (h + 1) * HS)
        part = 0.0
        for j in range(2):
            g = gf[h, 2 * j : 2 * j + 2].reshape(TEXT, HS)
            part = part + lax.dot_general(
                g, w_v[j, h], (((1,), (1,)), ((), ())), preferred_element_type=F32
            )
        part = part.reshape(NZ, NC, ZT, FEAT)
        if h == 0:
            tp[...] = part
        else:
            tp[...] += part
        if h == HEADS - 1:
            copy_to(tp.at[:, 1 - mc], tc, fs_sem.at[0], fr_sem.at[0], core_peer)
        for j, ref in enumerate((kwg_ref, vwg_ref)):
            wg = 0.0
            for a in range(2):
                wg = wg + dot(tt_v[a].reshape(FEAT, TH), gf[h, 2 * j + a].reshape(TH, HS))
            ref[:, cols] = wg

    for load in loads:
        load.wait()
    txt[mx] = tt_v[ma].reshape(FEAT, TH).T
    for h in range(HEADS):
        cols = slice(h * HS, (h + 1) * HS)
        qt_v[h] = q_v[:, cols].T
        ogt_v[h] = og_v[:, cols].T
    pl.semaphore_wait(barrier, len(peers))
    for i in (2, 1, 3):
        px, device = x_peer(i)
        copy_to(tt_v.at[lax.rem(px, 2), mc], tx.at[mx, mc], fs_sem.at[2], fr_sem.at[2], device)
    for h in range(HEADS):
        f_w(h)
    wait_bytes(fr_sem.at[2], tx.at[pl.ds(0, NX - 1), 0])
    for i in (1, 2, 3):
        px = x_peer(i)[0]
        copy_to(tx.at[px, mc], tx.at[px, mc], fs_sem.at[3], fr_sem.at[3], core_peer)
    wait_bytes(fr_sem.at[3], tx.at[pl.ds(0, NX - 1), 0])
    for i in range(1, NX):
        px = x_peer(i)[0]
        txt[px] = tx[px].reshape(FEAT, TH).T
    f_y(0)
    f_y(1)
    f_y(2)
    f_ay(0)
    f_ay(1)
    f_ay(2)
    f_ax(0)
    f_ax(1)
    f_ax(2)
    attend(0)
    attend(1)
    attend(2)
    b_y(0)
    b_y(1)
    b_ay(0)
    b_y(2)
    b_ay(1)
    b_ax(0)
    b_ay(2)
    b_ax(1)
    finish(0)
    b_ax(2)
    finish(1)
    finish(2)

    wait_bytes(fr_sem.at[0], tc)
    ts[...] = (tp[:, mc] + tc[...]).astype(BF)
    for i in FAR_FIRST:
        pz, device = z_peer(i)
        copy_to(ts.at[pz], tz.at[mz], fs_sem.at[1], fr_sem.at[1], device)
    for h in range(HEADS):
        for stage in range(8):
            wait(ssem, h, stage)
    wait_bytes(fs_sem.at[0], tc)
    wait_bytes(fs_sem.at[2], tx.at[pl.ds(0, NX - 1), 0])
    wait_bytes(fs_sem.at[3], tx.at[pl.ds(0, NX - 1), 0])
    wait_bytes(fr_sem.at[1], tz.at[pl.ds(0, NZ - 1)])
    t = tp[mz, mc] + tc[mz]
    for i in range(1, NZ):
        t = t + tz[z_peer(i)[0]].astype(F32)
    tg_ref[...] = t
    wait_bytes(fs_sem.at[1], tz.at[pl.ds(0, NZ - 1)])


def in_hbm(a):
    return pltpu.with_memory_space_constraint(a, pltpu.HBM)


def write_out(*refs):
    n = len(refs) // 2
    copies = [
        pltpu.make_async_copy(refs[i], refs[n + i], refs[-1].at[i]) for i in range(n)
    ]
    for copy in copies:
        copy.start()
    for copy in copies:
        copy.wait()


def local(queries, text, key_weight, value_weight, out_grad):
    width = HEADS * HS
    vm = pltpu.VMEM
    dma = pltpu.SemaphoreType.DMA
    held = pl.pallas_call(
        kernel,
        name="cross_attention",
        out_shape=(
            pltpu.VMEM((ROWS, width), BF),
            pltpu.VMEM((ROWS, width), BF),
            pltpu.VMEM((FEAT, width), F32),
            pltpu.VMEM((FEAT, width), F32),
            pltpu.VMEM((ZT, FEAT), F32),
        ),
        in_specs=[pl.BlockSpec(memory_space=pltpu.HBM)] * 5,
        out_specs=tuple([pl.BlockSpec(memory_space=pltpu.VMEM)] * 5),
        scratch_shapes=[
            vm((ROWS, width), BF), vm((ROWS, width), BF),
            vm((2, NC, FH, TH), BF), vm((2, HEADS, FEAT, HS), BF),
            vm((NX, NC, FH, TH), BF), vm((HEADS, NX, FEAT, HS), BF), vm((NX, TH, FEAT), BF),
            vm((HEADS, HS, ROWS), BF), vm((HEADS, HS, ROWS), BF),
            vm((HEADS, NY, YT, HS), F32), vm((HEADS, NY, YT, HS), F32),
            vm((HEADS, NX, NY, YT, HS), BF),
            vm((HEADS, NX, NY, YT, HS), BF), vm((HEADS, NX, NY, YT, HS), BF),
            vm((HEADS, NY, YT, HS), BF), vm((HEADS, NY, YT, HS), BF),
            vm((HEADS, NX, NY, YT, HS), BF),
            vm((NZ, NC, ZT, FEAT), F32), vm((NZ, ZT, FEAT), F32),
            vm((NZ, ZT, FEAT), BF), vm((NZ, ZT, FEAT), BF),
            dma((12,)), dma((HEADS, 8)), dma((HEADS, 8)), dma((4,)), dma((4,)),
        ],
        compiler_params=pltpu.CompilerParams(
            collective_id=0, has_side_effects=True, vmem_limit_bytes=48 * 1024 * 1024
        ),
    )(*(in_hbm(a) for a in (queries, text.T, key_weight, value_weight, out_grad)))
    return pl.pallas_call(
        write_out,
        name="write_out",
        out_shape=tuple(jax.ShapeDtypeStruct(a.shape, a.dtype) for a in held),
        in_specs=[pl.BlockSpec(memory_space=pltpu.VMEM)] * 5,
        out_specs=tuple([pl.BlockSpec(memory_space=pl.ANY)] * 5),
        scratch_shapes=[dma((5,))],
        compiler_params=pltpu.CompilerParams(vmem_limit_bytes=1024 * 1024),
    )(*held)


def solution(mesh):
    in_specs = (
        P("seq", "head"),
        P(None, "seq"),
        P("seq", "head"),
        P("seq", "head"),
        P("seq", "head"),
    )
    out_specs = (
        P("seq", "head"),
        P("seq", "head"),
        P("seq", "head"),
        P("seq", "head"),
        P("head", "seq"),
    )
    return jax.shard_map(local, mesh=mesh, in_specs=in_specs, out_specs=out_specs, check_vma=False)
```

time: 90.2 us -> 80.7 us (0.89)
  local copies, waits for them, and re-layouts: 5.73 us -> 0 us
  Pallas kernels: 83.5 us -> 79.9 us
    unnamed x13 -> x0, local copies, waits for them, and re-layouts: 5.73 us -> none
    pallas_call x1 -> x2, Pallas kernels: 83.5 us -> 79.9 us  [the longest x1 78.6 us: local(): pl.pallas_call(kernel, name='cross_attention', out_shape=(pltpu.VMEM((ROW...]
where the time goes in v2:
time: 80.7 us; the launch traced here: 80.6 us
  Pallas kernels  79.9 us (99%)
    pallas_call x1, Pallas kernels, local(): pl.pallas_call(kernel, name='cross_attention', out_shape=(pltpu.VMEM((ROW...  78.6 us

profile of v2, /device:TPU:1, one launch (start us, length us, event | category | flops | bytes accessed | tf_op | source)
XLA Modules:
  0.0 80.6 jit_solution(167642457093733989)
XLA Ops:
  0.6 78.6 %cross_attention.1 = (bf16[1024,384]{1,0:T(8,128)(2,1)S(1)}, bf16[1024,384]{1,0:T(8,128)(2,1)S(1)}, f32[192,384]{1,0:T(8,128)S(1)}, f32[192,384]{1,0:T(8,128)S(1)}, f32[32,192]{1,0:T(8,128)S(1)}) custom-call(bf16[1024,384]{1,0:T(8,128)(2,1)} %q_hbm.1, bf16[192,512]{1,0:T(8,128)(2,1)} %bitcast.1, bf16[192,384]{1,0:T(8,128)(2,1)} %kw_hbm.1, ...), custom_call_target="tpu_custom_call" | custom-call | tf_op jit(solution)/shard_map/cross_attention/pallas_call | solution.py:286
  79.2 1.4 %write_out.1 = (bf16[1024,384]{1,0:T(8,128)(2,1)}, bf16[1024,384]{1,0:T(8,128)(2,1)}, f32[192,384]{1,0:T(8,128)}, f32[192,384]{1,0:T(8,128)}, f32[32,192]{1,0:T(8,128)}) custom-call(bf16[1024,384]{1,0:T(8,128)(2,1)S(1)} %get-tuple-element.10.refs_0_, bf16[1024,384]{1,0:T(8,128)(2,1)S(1)} %get-tuple-element.11.refs_1_, ...), custom_call_target="tpu_custom_call" | custom-call | tf_op jit(solution)/shard_map/write_out/pallas_call | solution.py:316

commit v3 on v2

--- a/solution.py
+++ b/solution.py
@@ -11,6 +11,7 @@
 HEADS = 3
 TEXT = 512
 FEAT = 192
+WIDE = 256
 ROWS = 1024
 TH = TEXT // 2
 YT = TH // NY
@@ -23,6 +24,18 @@
 
 S_W, S_Y, S_AY, S_AX, S_GX, S_GY, S_GAY, S_GAX = range(8)
 FAR_FIRST = (4, 3, 5, 2, 6, 1, 7)
+
+
+def head_cols(h):
+    return pl.ds(pl.multiple_of(h * HS, HS), HS)
+
+
+def each(count, step):
+    def body(i, carry):
+        step(i)
+        return carry
+
+    lax.fori_loop(0, count, body, 0)
 
 
 def dot(a, b):
@@ -138,17 +151,17 @@
 
     def attend(h):
         wait(rsem, h, S_AX)
-        cols = slice(h * HS, (h + 1) * HS)
+        cols = head_cols(h)
         k = kvf[h, 0:2].reshape(TEXT, HS)
         v = kvf[h, 2:4].reshape(TEXT, HS)
         s = dot(k, qt_v[h])
         e = jnp.exp2((s - jnp.max(s, axis=0, keepdims=True)) * EXP2_SCALE)
         p = e * (1.0 / jnp.sum(e, axis=0, keepdims=True))
         low = p.astype(BF)
+        gp[h, 2:4] = dot(low, og_v[:, cols]).astype(BF).reshape(2, NY, YT, HS)
         dp = dot(v, ogt_v[h])
         delta = jnp.sum(p * dp, axis=0, keepdims=True)
         ds = (p * (dp - delta) * SCALE).astype(BF)
-        gp[h, 2:4] = dot(low, og_v[:, cols]).astype(BF).reshape(2, NY, YT, HS)
         gp[h, 0:2] = dot(ds, q_v[:, cols]).astype(BF).reshape(2, NY, YT, HS)
         for i in (2, 1, 3):
             px, device = x_peer(i)
@@ -179,39 +192,41 @@
 
     def finish(h):
         wait(rsem, h, S_GAX)
-        cols = slice(h * HS, (h + 1) * HS)
+        cols = head_cols(h)
         part = 0.0
         for j in range(2):
             g = gf[h, 2 * j : 2 * j + 2].reshape(TEXT, HS)
             part = part + lax.dot_general(
                 g, w_v[j, h], (((1,), (1,)), ((), ())), preferred_element_type=F32
             )
-        part = part.reshape(NZ, NC, ZT, FEAT)
-        if h == 0:
-            tp[...] = part
-        else:
-            tp[...] += part
-        if h == HEADS - 1:
+        tp[:, :, :, :FEAT] += part.reshape(NZ, NC, ZT, FEAT)
+
+        @pl.when(h == HEADS - 1)
+        def _():
             copy_to(tp.at[:, 1 - mc], tc, fs_sem.at[0], fr_sem.at[0], core_peer)
+
         for j, ref in enumerate((kwg_ref, vwg_ref)):
             wg = 0.0
             for a in range(2):
                 wg = wg + dot(tt_v[a].reshape(FEAT, TH), gf[h, 2 * j + a].reshape(TH, HS))
             ref[:, cols] = wg
 
+    tp[...] = jnp.zeros_like(tp)
     for load in loads:
         load.wait()
     txt[mx] = tt_v[ma].reshape(FEAT, TH).T
-    for h in range(HEADS):
-        cols = slice(h * HS, (h + 1) * HS)
+
+    def turn(h):
+        cols = head_cols(h)
         qt_v[h] = q_v[:, cols].T
         ogt_v[h] = og_v[:, cols].T
+
+    pl.when(mc == 0)(lambda: each(HEADS, turn))
     pl.semaphore_wait(barrier, len(peers))
     for i in (2, 1, 3):
         px, device = x_peer(i)
         copy_to(tt_v.at[lax.rem(px, 2), mc], tx.at[mx, mc], fs_sem.at[2], fr_sem.at[2], device)
-    for h in range(HEADS):
-        f_w(h)
+    pl.when(mc == 0)(lambda: each(HEADS, f_w))
     wait_bytes(fr_sem.at[2], tx.at[pl.ds(0, NX - 1), 0])
     for i in (1, 2, 3):
         px = x_peer(i)[0]
@@ -220,39 +235,38 @@
     for i in range(1, NX):
         px = x_peer(i)[0]
         txt[px] = tx[px].reshape(FEAT, TH).T
-    f_y(0)
-    f_y(1)
-    f_y(2)
-    f_ay(0)
-    f_ay(1)
-    f_ay(2)
-    f_ax(0)
-    f_ax(1)
-    f_ax(2)
-    attend(0)
-    attend(1)
-    attend(2)
-    b_y(0)
-    b_y(1)
-    b_ay(0)
-    b_y(2)
-    b_ay(1)
-    b_ax(0)
-    b_ay(2)
-    b_ax(1)
-    finish(0)
-    b_ax(2)
-    finish(1)
-    finish(2)
+
+    def gather(i):
+        pl.when(i < HEADS)(lambda: f_ay(i))
+        pl.when(i >= 1)(lambda: f_ax(i - 1))
+
+    def grads(i):
+        pl.when(i < HEADS)(lambda: b_y(i))
+        pl.when((i >= 1) & (i <= HEADS))(lambda: b_ay(i - 1))
+        pl.when(i >= 2)(lambda: b_ax(i - 2))
+
+    @pl.when(mc == 1)
+    def _():
+        each(HEADS, turn)
+        each(HEADS, f_w)
+
+    each(HEADS, f_y)
+    each(HEADS + 1, gather)
+    each(HEADS, attend)
+    each(HEADS + 2, grads)
+    each(HEADS, finish)
 
     wait_bytes(fr_sem.at[0], tc)
     ts[...] = (tp[:, mc] + tc[...]).astype(BF)
     for i in FAR_FIRST:
         pz, device = z_peer(i)
         copy_to(ts.at[pz], tz.at[mz], fs_sem.at[1], fr_sem.at[1], device)
-    for h in range(HEADS):
+
+    def sent(h):
         for stage in range(8):
             wait(ssem, h, stage)
+
+    each(HEADS, sent)
     wait_bytes(fs_sem.at[0], tc)
     wait_bytes(fs_sem.at[2], tx.at[pl.ds(0, NX - 1), 0])
     wait_bytes(fs_sem.at[3], tx.at[pl.ds(0, NX - 1), 0])
@@ -260,7 +274,7 @@
     t = tp[mz, mc] + tc[mz]
     for i in range(1, NZ):
         t = t + tz[z_peer(i)[0]].astype(F32)
-    tg_ref[...] = t
+    tg_ref[...] = t[:, :FEAT]
     wait_bytes(fs_sem.at[1], tz.at[pl.ds(0, NZ - 1)])
 
 
@@ -305,8 +319,8 @@
             vm((HEADS, NX, NY, YT, HS), BF), vm((HEADS, NX, NY, YT, HS), BF),
             vm((HEADS, NY, YT, HS), BF), vm((HEADS, NY, YT, HS), BF),
             vm((HEADS, NX, NY, YT, HS), BF),
-            vm((NZ, NC, ZT, FEAT), F32), vm((NZ, ZT, FEAT), F32),
-            vm((NZ, ZT, FEAT), BF), vm((NZ, ZT, FEAT), BF),
+            vm((NZ, NC, ZT, WIDE), F32), vm((NZ, ZT, WIDE), F32),
+            vm((NZ, ZT, WIDE), BF), vm((NZ, ZT, WIDE), BF),
             dma((12,)), dma((HEADS, 8)), dma((HEADS, 8)), dma((4,)), dma((4,)),
         ],
         compiler_params=pltpu.CompilerParams(

time: 80.7 us -> 76.3 us (0.945)
  Pallas kernels: 79.9 us -> 75.5 us
    pallas_call x1, Pallas kernels: 78.6 us -> 74.1 us  [local(): pl.pallas_call(kernel, name='cross_attention', out_shape=(pltpu.VMEM((ROW...]
where the time goes in v3:
time: 76.3 us; the launch traced here: 76.1 us
  Pallas kernels  75.5 us (99%)
    pallas_call x1, Pallas kernels, local(): pl.pallas_call(kernel, name='cross_attention', out_shape=(pltpu.VMEM((ROW...  74.1 us

profile of v3, /device:TPU:1, one launch (start us, length us, event | category | flops | bytes accessed | tf_op | source)
XLA Modules:
  0.0 76.1 jit_solution(15080958814726823417)
XLA Ops:
  0.6 74.1 %cross_attention.1 = (bf16[1024,384]{1,0:T(8,128)(2,1)S(1)}, bf16[1024,384]{1,0:T(8,128)(2,1)S(1)}, f32[192,384]{1,0:T(8,128)S(1)}, f32[192,384]{1,0:T(8,128)S(1)}, f32[32,192]{1,0:T(8,128)S(1)}) custom-call(bf16[1024,384]{1,0:T(8,128)(2,1)} %q_hbm.1, bf16[192,512]{1,0:T(8,128)(2,1)} %bitcast.1, bf16[192,384]{1,0:T(8,128)(2,1)} %kw_hbm.1, ...), custom_call_target="tpu_custom_call" | custom-call | tf_op jit(solution)/shard_map/cross_attention/pallas_call | solution.py:300
  74.7 1.4 %write_out.1 = (bf16[1024,384]{1,0:T(8,128)(2,1)}, bf16[1024,384]{1,0:T(8,128)(2,1)}, f32[192,384]{1,0:T(8,128)}, f32[192,384]{1,0:T(8,128)}, f32[32,192]{1,0:T(8,128)}) custom-call(bf16[1024,384]{1,0:T(8,128)(2,1)S(1)} %get-tuple-element.10.refs_0_, bf16[1024,384]{1,0:T(8,128)(2,1)S(1)} %get-tuple-element.11.refs_1_, ...), custom_call_target="tpu_custom_call" | custom-call | tf_op jit(solution)/shard_map/write_out/pallas_call | solution.py:330

commit v4 on v3

--- a/solution.py
+++ b/solution.py
@@ -245,12 +245,12 @@
         pl.when((i >= 1) & (i <= HEADS))(lambda: b_ay(i - 1))
         pl.when(i >= 2)(lambda: b_ax(i - 2))
 
-    @pl.when(mc == 1)
-    def _():
-        each(HEADS, turn)
-        each(HEADS, f_w)
-
-    each(HEADS, f_y)
+    def weights_and_sums(h):
+        pl.when(mc == 1)(lambda: f_w(h))
+        f_y(h)
+
+    pl.when(mc == 1)(lambda: each(HEADS, turn))
+    each(HEADS, weights_and_sums)
     each(HEADS + 1, gather)
     each(HEADS, attend)
     each(HEADS + 2, grads)

time: 76.3 us -> 75.4 us (0.988)
  Pallas kernels: 75.5 us -> 74.6 us
    pallas_call x1, Pallas kernels: 74.1 us -> 73.2 us  [local(): pl.pallas_call(kernel, name='cross_attention', out_shape=(pltpu.VMEM((ROW...]
where the time goes in v4:
time: 75.4 us; the launch traced here: 75.3 us
  Pallas kernels  74.6 us (99%)
    pallas_call x1, Pallas kernels, local(): pl.pallas_call(kernel, name='cross_attention', out_shape=(pltpu.VMEM((ROW...  73.2 us

profile of v4, /device:TPU:1, one launch (start us, length us, event | category | flops | bytes accessed | tf_op | source)
XLA Modules:
  0.0 75.3 jit_solution(2352783672969962943)
XLA Ops:
  0.6 73.2 %cross_attention.1 = (bf16[1024,384]{1,0:T(8,128)(2,1)S(1)}, bf16[1024,384]{1,0:T(8,128)(2,1)S(1)}, f32[192,384]{1,0:T(8,128)S(1)}, f32[192,384]{1,0:T(8,128)S(1)}, f32[32,192]{1,0:T(8,128)S(1)}) custom-call(bf16[1024,384]{1,0:T(8,128)(2,1)} %q_hbm.1, bf16[192,512]{1,0:T(8,128)(2,1)} %bitcast.1, bf16[192,384]{1,0:T(8,128)(2,1)} %kw_hbm.1, ...), custom_call_target="tpu_custom_call" | custom-call | tf_op jit(solution)/shard_map/cross_attention/pallas_call | solution.py:300
  73.9 1.4 %write_out.1 = (bf16[1024,384]{1,0:T(8,128)(2,1)}, bf16[1024,384]{1,0:T(8,128)(2,1)}, f32[192,384]{1,0:T(8,128)}, f32[192,384]{1,0:T(8,128)}, f32[32,192]{1,0:T(8,128)}) custom-call(bf16[1024,384]{1,0:T(8,128)(2,1)S(1)} %get-tuple-element.10.refs_0_, bf16[1024,384]{1,0:T(8,128)(2,1)S(1)} %get-tuple-element.11.refs_1_, ...), custom_call_target="tpu_custom_call" | custom-call | tf_op jit(solution)/shard_map/write_out/pallas_call | solution.py:330

commit v5 on v4

--- a/solution.py
+++ b/solution.py
@@ -163,11 +163,16 @@
         delta = jnp.sum(p * dp, axis=0, keepdims=True)
         ds = (p * (dp - delta) * SCALE).astype(BF)
         gp[h, 0:2] = dot(ds, q_v[:, cols]).astype(BF).reshape(2, NY, YT, HS)
-        for i in (2, 1, 3):
-            px, device = x_peer(i)
-            send(gp.at[h, px], gx.at[h, mx], h, S_GX, device)
+
+        def send_grads():
+            for i in (2, 1, 3):
+                px, device = x_peer(i)
+                send(gp.at[h, px], gx.at[h, mx], h, S_GX, device)
+
+        pl.when(mc == 0)(send_grads)
         o_ref[:, cols] = dot(v.T, low).T.astype(BF)
         dq_ref[:, cols] = dot(k.T, ds).T.astype(BF)
+        pl.when(mc == 1)(send_grads)
 
     def b_y(h):
         wait(rsem, h, S_GX)

time: 75.4 us -> 75.4 us (level)
  no operation moved by 1% of the time
where the time goes in v5:
time: 75.4 us; the launch traced here: 75.2 us
  Pallas kernels  74.6 us (99%)
    pallas_call x1, Pallas kernels, local(): pl.pallas_call(kernel, name='cross_attention', out_shape=(pltpu.VMEM((ROW...  73.2 us

profile of v5, /device:TPU:1, one launch (start us, length us, event | category | flops | bytes accessed | tf_op | source)
XLA Modules:
  0.0 75.2 jit_solution(12996185244842824799)
XLA Ops:
  0.6 73.2 %cross_attention.1 = (bf16[1024,384]{1,0:T(8,128)(2,1)S(1)}, bf16[1024,384]{1,0:T(8,128)(2,1)S(1)}, f32[192,384]{1,0:T(8,128)S(1)}, f32[192,384]{1,0:T(8,128)S(1)}, f32[32,192]{1,0:T(8,128)S(1)}) custom-call(bf16[1024,384]{1,0:T(8,128)(2,1)} %q_hbm.1, bf16[192,512]{1,0:T(8,128)(2,1)} %bitcast.1, bf16[192,384]{1,0:T(8,128)(2,1)} %kw_hbm.1, ...), custom_call_target="tpu_custom_call" | custom-call | tf_op jit(solution)/shard_map/cross_attention/pallas_call | solution.py:305
  73.8 1.4 %write_out.1 = (bf16[1024,384]{1,0:T(8,128)(2,1)}, bf16[1024,384]{1,0:T(8,128)(2,1)}, f32[192,384]{1,0:T(8,128)}, f32[192,384]{1,0:T(8,128)}, f32[32,192]{1,0:T(8,128)}) custom-call(bf16[1024,384]{1,0:T(8,128)(2,1)S(1)} %get-tuple-element.10.refs_0_, bf16[1024,384]{1,0:T(8,128)(2,1)S(1)} %get-tuple-element.11.refs_1_, ...), custom_call_target="tpu_custom_call" | custom-call | tf_op jit(solution)/shard_map/write_out/pallas_call | solution.py:335
